TPU v7x, 256 devices: a whole 4x4x8 slice. The times are simulated.
256 devices in a mesh: row: 16 (over x, z_lo), col: 4 (over y), depth: 4 (over z_hi, core).
Axes of the slice: x: 4, y: 4, z: 8 (z_hi: 2, z_lo: 4; z = z_hi * 4 + z_lo), core: 2. Of those that a mesh axis runs over, the one named last changes fastest.
Arguments:
- features: bfloat16 [65536, 512], P(('row', 'col'), 'depth'), may hold values from -6 to 6
- weight: bfloat16 [512, 512], replicated, may hold values from -0.25 to 0.25
- cotangent: bfloat16 [65536, 512], P(('row', 'col'), 'depth'), may hold values from -6 to 6
- adjacency_blocks: bfloat16 [16, 4, 80, 256, 256], P('row', 'col'), may hold values from -0.078125 to 0.078125
- block_rows: int32 [16, 4, 80], P('row', 'col'), may hold values from 0 to 15, as said below
- block_cols: int32 [16, 4, 80], P('row', 'col'), may hold values from 0 to 63
- tile_counts: int32 [16, 4], P('row', 'col'), may hold values from 20 to 80, as said below
Outputs:
- activated: bfloat16 [65536, 512], P(('row', 'col'), 'depth')
- grad_features: bfloat16 [65536, 512], P(('row', 'col'), 'depth')
- grad_weight: float32 [512, 512], P('depth')
Inputs may be any that keep to these rules, and one draw needn't show every extreme that they name: Within one tile the pairs (block_rows, block_cols) of its 80 slots are all different. `tile_counts`: some tile uses all 80 slots.
All inputs are finite; a program needn't handle non-finite values.
Results may differ from a plain program's by a relative error of at most 0.029.
Values may be sent and summed in bfloat16 or wider, within the bound.
A program may use at most 64 MiB of HBM per device.

v0:
```python
import jax
import jax.numpy as jnp
from jax import lax
from jax.sharding import PartitionSpec as P


def activate(values):
    return jax.nn.gelu(values, approximate=True)


def on_device(features, weight, cotangent, adjacency_blocks, block_rows, block_cols, tile_counts):
    blocks = adjacency_blocks[0, 0]
    rows_of = block_rows[0, 0]
    cols_of = block_cols[0, 0]
    tile_count = tile_counts[0, 0]
    rows_dev, feat_width = features.shape
    block_size = blocks.shape[-1]
    slots = blocks.shape[0]
    row_blocks = lax.axis_size("col") * rows_dev // block_size
    usable = (jnp.arange(slots) < tile_count).astype(jnp.float32)
    gathered = lax.all_gather(features, "row", axis=0, tiled=True)
    col_blocks = gathered.shape[0] // block_size
    source = gathered.reshape(col_blocks, block_size, feat_width)
    picked = source[cols_of]
    products = jnp.einsum("nij,njf->nif", blocks, picked, preferred_element_type=jnp.float32)
    placing = (rows_of[None, :] == jnp.arange(row_blocks)[:, None]).astype(jnp.float32) * usable[
        None, :
    ]
    partial_sum = jnp.einsum("rn,nif->rif", placing, products).reshape(
        row_blocks * block_size, feat_width
    )
    aggregated = lax.psum_scatter(
        partial_sum.astype(jnp.bfloat16), "col", scatter_dimension=0, tiled=True
    )
    depth_index = lax.axis_index("depth")
    rows_part = lax.dynamic_slice_in_dim(weight, depth_index * feat_width, feat_width, 0)
    terms = jnp.dot(aggregated, rows_part, preferred_element_type=jnp.float32)
    mixed = lax.psum_scatter(
        terms.astype(jnp.bfloat16), "depth", scatter_dimension=1, tiled=True
    ).astype(jnp.float32)
    activated = activate(mixed).astype(jnp.bfloat16)
    _, pullback = jax.vjp(activate, mixed)
    grad_mixed = pullback(cotangent.astype(jnp.float32))[0].astype(jnp.bfloat16)
    grad_full = lax.all_gather(grad_mixed, "depth", axis=1, tiled=True)
    weight_part = lax.dot_general(
        aggregated, grad_full, (((0,), (0,)), ((), ())), preferred_element_type=jnp.float32
    )
    grad_weight = lax.psum(weight_part, ("row", "col"))
    grad_aggregated = lax.dot_general(
        grad_full, rows_part, (((1,), (1,)), ((), ())), preferred_element_type=jnp.float32
    ).astype(jnp.bfloat16)
    target_rows = lax.all_gather(grad_aggregated, "col", axis=0, tiled=True).reshape(
        row_blocks, block_size, feat_width
    )
    picked_back = target_rows[rows_of]
    products_back = jnp.einsum(
        "nij,nif->njf", blocks, picked_back, preferred_element_type=jnp.float32
    )
    placing_back = (cols_of[None, :] == jnp.arange(col_blocks)[:, None]).astype(
        jnp.float32
    ) * usable[None, :]
    terms_back = jnp.einsum("cn,njf->cjf", placing_back, products_back).reshape(
        col_blocks * block_size, feat_width
    )
    grad_source = lax.psum_scatter(
        terms_back.astype(jnp.bfloat16), "row", scatter_dimension=0, tiled=True
    )
    return (activated, grad_source, grad_weight)


def solution(mesh):
    in_specs = (
        P(("row", "col"), "depth"),
        P(),
        P(("row", "col"), "depth"),
        P("row", "col", None, None, None),
        P("row", "col", None),
        P("row", "col", None),
        P("row", "col"),
    )
    out_specs = (P(("row", "col"), "depth"), P(("row", "col"), "depth"), P("depth", None))
    return jax.shard_map(
        on_device, mesh=mesh, in_specs=in_specs, out_specs=out_specs, check_vma=False
    )
```

profile of v0, /device:TPU:8, one launch (start us, length us, event | category | flops | bytes accessed | tf_op | source)
XLA Modules:
  0.0 1042.3 jit_solution(14566805836173315483)
XLA Ops:
  7.2 0.7 all-gather.4.cloned.1.call-update
  7.9 0.0 reduce-scatter.6.cloned.1.call-start
  8.6 0.7 fusion.33
  9.3 105.4 %all-gather.4.cloned.1.call-done = bf16[16384,128]{1,0:T(8,128)(2,1)} async-done(((bf16[1024,128]{1,0:T(8,128)(2,1)}), bf16[16384,128]{1,0:T(8,128)(2,1)}) %all-gather.4.cloned.1.call-update) | async-done | bytes 4194320 | tf_op jit(solution)/shard_map/all_gather | solution.py:21
  114.7 7.8 gather_fusion
  122.5 8.8 fusion.4
  131.3 8.6 copy.17
  139.9 3.3 convolution_convert_fusion.1
  143.2 1.3 copy.18
  144.5 0.0 reduce-scatter.10.cloned.1.call-start
  144.5 21.5 %reduce-scatter.6.cloned.1.call-done = bf16[1024,128]{1,0:T(8,128)(2,1)} async-done(((bf16[4096,128]{1,0:T(8,128)(2,1)}), bf16[1024,128]{1,0:T(8,128)(2,1)}) %reduce-scatter.6.cloned.1.call-update) | async-done | bytes 262160 | tf_op jit(solution)/shard_map/reduce_scatter | solution.py:32
  166.0 1.4 convolution_convert_fusion.2
  167.5 1.3 copy.24
  168.8 0.0 all-gather.6.cloned.1.call-start
  168.9 47.3 %reduce-scatter.10.cloned.1.call-done = bf16[128,1024]{1,0:T(8,128)(2,1)} async-done(((bf16[512,1024]{1,0:T(8,128)(2,1)}), bf16[128,1024]{1,0:T(8,128)(2,1)}) %reduce-scatter.10.cloned.1.call-update) | async-done | bytes 262160
  216.1 1.1 copy.25
  217.3 1.2 fusion.13
  218.5 0.0 all-gather.8.cloned.1.call-start
  218.5 28.1 %all-gather.6.cloned.1.call-done = bf16[1024,512]{1,0:T(8,128)(2,1)} async-done(((bf16[1024,128]{1,0:T(8,128)(2,1)}), bf16[1024,512]{1,0:T(8,128)(2,1)}) %all-gather.6.cloned.1.call-update) | async-done | bytes 1048592 | tf_op jit(solution)/shard_map/all_gather | solution.py:44
  246.7 2.4 convolution_convert_fusion.3
  249.1 0.0 all-reduce.2.cloned.1.call-start
  249.1 2.3 fusion.39
  251.4 0.2 reduce-scatter.8.cloned.1.call-start
  251.7 19.4 %all-gather.8.cloned.1.call-done = bf16[4096,128]{1,0:T(8,128)(2,1)} async-done(((bf16[1024,128]{1,0:T(8,128)(2,1)}), bf16[4096,128]{1,0:T(8,128)(2,1)}) %all-gather.8.cloned.1.call-update) | async-done | bytes 1048592 | tf_op jit(solution)/shard_map/all_gather | solution.py:52
  271.0 6.9 gather_fusion.1
  277.9 9.8 fusion.7
  287.7 8.6 copy.20
  296.2 3.7 convolution_convert_fusion
  300.0 4.7 copy.21
  304.7 624.4 %all-reduce.2.cloned.1.call-done = f32[128,512]{1,0:T(8,128)} async-done(((f32[128,512]{1,0:T(8,128)}), f32[128,512]{1,0:T(8,128)}) %all-reduce.2.cloned.1.call-update) | async-done | bytes 262160 | tf_op jit(solution)/shard_map/psum | solution.py:48
  929.0 104.7 %reduce-scatter.8.cloned.1.call-done = bf16[1024,128]{1,0:T(8,128)(2,1)} async-done(((bf16[16384,128]{1,0:T(8,128)(2,1)}), bf16[1024,128]{1,0:T(8,128)(2,1)}) %reduce-scatter.8.cloned.1.call-update) | async-done | bytes 262160 | tf_op jit(solution)/shard_map/reduce_scatter | solution.py:65
  1033.7 1.7 copy.28
  (21 shorter events, 0.2 us)
Async XLA Ops:
  7.2 158.9 %copy-start = (bf16[512,512]{1,0:T(8,128)(2,1)S(1)}, bf16[512,512]{1,0:T(8,128)(2,1)}, u32[]{:S(2)}) copy-start(bf16[512,512]{1,0:T(8,128)(2,1)} %param.8) | copy-start | bytes 1572868
  7.2 107.5 %all-gather.4.cloned.1.call-start = ((), (), s32[]{:S(2)}) async-start(), calls=%async_computation.3 | async-start | bytes 4456448 | tf_op jit(solution)/shard_map/all_gather | solution.py:21
  7.9 158.1 %reduce-scatter.6.cloned.1.call-start = ((), (), s32[]{:S(2)}) async-start(), calls=%async_computation.4 | async-start | bytes 1310720 | tf_op jit(solution)/shard_map/reduce_scatter | solution.py:32
  131.3 8.6 copy-start.4
  143.2 74.0 %copy-start.2 = (bf16[1024,128]{1,0:T(8,128)(2,1)S(1)}, bf16[1024,128]{1,0:T(8,128)(2,1)}, u32[]{:S(2)}) copy-start(bf16[1024,128]{1,0:T(8,128)(2,1)} %param.9) | copy-start | bytes 786436
  144.5 71.6 %reduce-scatter.10.cloned.1.call-start = ((), (), s32[]{:S(2)}) async-start(), calls=%async_computation.9 | async-start | bytes 1310720
  166.0 83.1 %copy-start.1 = (bf16[1024,128]{1,0:T(8,128)(2,1)S(1)}, bf16[1024,128]{1,0:T(8,128)(2,1)}, u32[]{:S(2)}) copy-start(bf16[1024,128]{1,0:T(8,128)(2,1)} %reduce-scatter.6.cloned.1.call-done) | copy-start | bytes 786436
  168.8 77.9 %all-gather.6.cloned.1.call-start = ((), (), s32[]{:S(2)}) async-start(), calls=%async_computation.5 | async-start | bytes 1310720 | tf_op jit(solution)/shard_map/all_gather | solution.py:44
  218.5 52.5 %all-gather.8.cloned.1.call-start = ((), (), s32[]{:S(2)}) async-start(), calls=%async_computation.6 | async-start | bytes 1310720 | tf_op jit(solution)/shard_map/all_gather | solution.py:52
  249.1 680.0 %all-reduce.2.cloned.1.call-start = ((), (), s32[]{:S(2)}) async-start(), calls=%async_computation.8 | async-start | bytes 524288 | tf_op jit(solution)/shard_map/psum | solution.py:48
  251.4 782.3 %reduce-scatter.8.cloned.1.call-start = ((), (), s32[]{:S(2)}) async-start(), calls=%async_computation.7 | async-start | bytes 4456448 | tf_op jit(solution)/shard_map/reduce_scatter | solution.py:65
  287.6 8.6 copy-start.3
Sparse Core Ops, SparseCore 0:
  9.8 104.8 all-gather.3
  144.6 21.3 reduce-scatter.5
  169.0 47.0 reduce-scatter.9
  218.6 28.0 all-gather.5
  249.2 21.7 all-gather.7
  274.1 654.9 all-reduce.1
  932.3 101.3 reduce-scatter.7
where the time goes:
time: 1040 us
  waiting for transfers between devices  951 us (91%)
  local copies, waits for them, and re-layouts  41.9 us (4%)
  matrix products  31.7 us (3%)
  between operations  14.9 us (1%)
    psum x1, waiting for transfers between devices, on_device(): grad_weight = lax.psum(weight_part, ('row', 'col'))  624 us
    all_gather x1, waiting for transfers between devices, on_device(): gathered = lax.all_gather(features, 'row', axis=0, tiled=True)  105 us
    reduce_scatter x1, waiting for transfers between devices, on_device(): lax.psum_scatter(terms_back.astype(jnp.bfloat16), 'row', scatter_dimensio...  105 us
    unnamed x8, waiting for transfers between devices  48 us
    all_gather x1, waiting for transfers between devices, on_device(): grad_full = lax.all_gather(grad_mixed, 'depth', axis=1, tiled=True)  28.1 us
    reduce_scatter x1, waiting for transfers between devices, on_device(): lax.psum_scatter(partial_sum.astype(jnp.bfloat16), 'col', scatter_dimensi...  21.5 us
  transfers between devices with their start and end apart: 7, of which 7 were waited for; matrix products, arithmetic and copies ran while one was open for 4% of the time, Pallas kernels for 0%

commit v1 on v0

v1 whole, which is shorter than its diff:
```python
import functools

import jax
import jax.numpy as jnp
from jax import lax
from jax.experimental import pallas as pl
from jax.experimental.pallas import tpu as pltpu
from jax.sharding import PartitionSpec as P

BF = jnp.bfloat16
F32 = jnp.float32
K = 4
CH = 32
BS = 256
FS = 128
GC = 0.7978845608028654
NB = 80
PF, CF, KF, LF = 0, 80, 160, 240
PB, RB, KB, LB = 256, 336, 416, 496


def sorted_slots(major, minor, span, valid, groups):
    slots = major.shape[0]
    at = jnp.arange(slots)
    key = jnp.where(valid, major * span + minor, 4096 + at)
    rank = jnp.sum((key[None, :] < key[:, None]).astype(jnp.int32), axis=1)
    hit = (rank[None, :] == at[:, None]).astype(jnp.int32)
    perm = jnp.sum(hit * at[None, :], axis=1)
    minor_sorted = jnp.sum(hit * minor[None, :], axis=1)
    major_sorted = jnp.sum(hit * major[None, :], axis=1)
    before = jnp.concatenate([jnp.full((1,), -1, jnp.int32), major_sorted[:-1]])
    keep = (major_sorted == before).astype(jnp.int32)
    g = jnp.arange(groups)
    ends = jnp.sum((valid[None, :] & (major[None, :] <= g[:, None])).astype(jnp.int32), axis=1)
    used = jnp.any(valid[None, :] & (major[None, :] == g[:, None]), axis=1)
    last = jnp.where(used, ends - 1, -1)
    return [perm, minor_sorted, keep, last]


def kernel(
    idx, feat, weight, cot, adj_hbm,
    act_out, gf_out, gw_out,
    adj, gath, work, buf, part, yrecv, agg, cott, gmix, wt, actt,
    tgt, terms, xfl, xfr, xol, xor_, lines, zfd, zfu, fin,
    gw, gwy, gwx, gwxr, gwz, gwxa,
    adj_sem,
    zsu, zsd, zr, xsr, xsl, xrl, xrr, osr, osl, orl, orr,
    ys, yr, ds, dr, cs, cr, gs, gr, ts, tr,
    asr, asl, arl, arr, bsr, bsl, brl, brr, us, dns, ur, dnr,
    wys, wyr, wxs, wxr, wzs, wzr, vxs, vxr, vys, vyr,
):
    row = lax.axis_index("row")
    c = lax.axis_index("col")
    d = lax.axis_index("depth")
    x, z = row // 4, row % 4
    zh, core = d // 2, d % 2
    right = {"row": (x + 1) % 4 * 4 + z}
    left = {"row": (x + 3) % 4 * 4 + z}
    up = {"row": x * 4 + (z + 1) % 4}
    down = {"row": x * 4 + (z + 3) % 4}
    d_core = zh * 2 + (1 - core)
    d_far = (1 - zh) * 2 + core
    d_diag = (1 - zh) * 2 + (1 - core)
    to_core = {"depth": d_core}
    to_far = {"depth": d_far}
    xr1, xl1, xop = (x + 1) % 4, (x + 3) % 4, (x + 2) % 4

    def rcopy(src, dst, ssem, rsem, dev):
        return pltpu.make_async_remote_copy(
            src_ref=src, dst_ref=dst, send_sem=ssem, recv_sem=rsem,
            device_id=dev, device_id_type=pl.DeviceIdType.MESH,
        )

    def go(op, *args):
        copy = rcopy(*args)
        if op == "start":
            copy.start()
        elif op == "sent":
            copy.wait_send()
        else:
            copy.wait_recv()

    barrier = pltpu.get_barrier_semaphore()
    for o in range(1, 4):
        for dev in (
            {"row": (x + o) % 4 * 4 + z},
            {"row": x * 4 + (z + o) % 4},
            {"col": (c + o) % 4},
        ):
            pl.semaphore_signal(barrier, inc=1, device_id=dev, device_id_type=pl.DeviceIdType.MESH)
    for dev in (to_core, to_far):
        pl.semaphore_signal(barrier, inc=1, device_id=dev, device_id_type=pl.DeviceIdType.MESH)

    adj_copy = pltpu.make_async_copy(adj_hbm, adj, adj_sem)
    adj_copy.start()

    for b in range(4):
        flip = feat[b * BS:(b + 1) * BS, :].astype(F32).T.astype(BF)
        for k in range(K):
            gath[k, row * 4 + b] = flip[k * CH:(k + 1) * CH]

    pl.semaphore_wait(barrier, 11)

    def shard(k, xx, zz):
        return gath.at[k, pl.ds((xx * 4 + zz) * 4, 4)]

    def lower(k, xx, zz):
        return gath.at[k, pl.ds((xx * 4 + zz) * 4, 2)]

    def upper(k, xx, zz):
        return gath.at[k, pl.ds((xx * 4 + zz) * 4 + 2, 2)]

    def z_up(op, k, zz):
        go(op, shard(k, x, zz), shard(k, x, zz), zsu.at[k, zz], zr.at[k, zz], up)

    def z_down(op, k, zz):
        go(op, shard(k, x, zz), shard(k, x, zz), zsd.at[k, zz], zr.at[k, zz], down)

    def z_own(op, k):
        @pl.when(z < 3)
        def _():
            z_up(op, k, z)

        @pl.when(z > 0)
        def _():
            z_down(op, k, z)

    def x_send(op, k, zz):
        go(op, shard(k, x, zz), shard(k, x, zz), xsr.at[k, zz], xrl.at[k, zz], right)
        go(op, shard(k, x, zz), shard(k, x, zz), xsl.at[k, zz], xrr.at[k, zz], left)

    def z_stage(op, k):
        for o in range(1, 4):
            @pl.when(z >= o)
            def _():
                zz = z - o
                if op == "start":
                    z_up("recv", k, zz)

                @pl.when(z < 3)
                def _():
                    z_up(op, k, zz)
                x_send(op, k, zz)

            @pl.when(z + o <= 3)
            def _():
                zz = z + o
                if op == "start":
                    z_down("recv", k, zz)

                @pl.when(z > 0)
                def _():
                    z_down(op, k, zz)
                x_send(op, k, zz)

    def x_pass(op, k):
        def one(i, _):
            zz = (z + i) % 4
            if op == "start":
                go("recv", shard(k, xl1, zz), shard(k, xl1, zz), xsr.at[k, zz], xrl.at[k, zz], right)
            go(op, lower(k, xl1, zz), lower(k, xl1, zz), osr.at[k, zz], orl.at[k, zz], right)
            if op == "start":
                go("recv", shard(k, xr1, zz), shard(k, xr1, zz), xsl.at[k, zz], xrr.at[k, zz], left)
            go(op, upper(k, xr1, zz), upper(k, xr1, zz), osl.at[k, zz], orr.at[k, zz], left)
            return 0
        lax.fori_loop(0, 4, one, 0)

    def x_last(k):
        def one(i, _):
            zz = (z + i) % 4
            go("recv", lower(k, xop, zz), lower(k, xop, zz), osr.at[k, zz], orl.at[k, zz], right)
            go("recv", upper(k, xop, zz), upper(k, xop, zz), osl.at[k, zz], orr.at[k, zz], left)
            return 0
        lax.fori_loop(0, 4, one, 0)

    def y_send(op, k):
        for o in range(1, 4):
            to = (c + o) % 4
            go(op, part.at[k, pl.ds(to * 4, 4)], yrecv.at[k, c], ys.at[k, o], yr.at[k, c], {"col": to})

    def y_sum(k):
        for o in range(1, 4):
            src = (c + o) % 4
            go("recv", part.at[k, pl.ds(c * 4, 4)], yrecv.at[k, src], ys.at[k, o], yr.at[k, src], {"col": src})
        for b in range(4):
            total = part[k, c * 4 + b].astype(F32)
            for o in range(1, 4):
                total = total + yrecv[k, (c + o) % 4, b].astype(F32)
            agg[b, pl.ds(pl.multiple_of(d * FS + k * CH, CH), CH), :] = total.astype(BF)

    def agg_rows(dd, k):
        return agg.at[:, pl.ds(pl.multiple_of(dd * FS + k * CH, CH), CH), :]

    def d_send(op, k):
        go(op, agg_rows(d, k), agg_rows(d, k), ds.at[k, 1], dr.at[k, 1], to_far)
        go(op, agg_rows(d, k), agg_rows(d, k), ds.at[k, 0], dr.at[k, 0], to_core)

    def d_pass(op, k):
        if op == "start":
            go("recv", agg_rows(d_far, k), agg_rows(d_far, k), ds.at[k, 1], dr.at[k, 1], to_far)
        go(op, agg_rows(d_far, k), agg_rows(d_far, k), ds.at[k, 2], dr.at[k, 2], to_core)

    def d_last(k):
        go("recv", agg_rows(d_core, k), agg_rows(d_core, k), ds.at[k, 0], dr.at[k, 0], to_core)
        go("recv", agg_rows(d_diag, k), agg_rows(d_diag, k), ds.at[k, 2], dr.at[k, 2], to_core)

    def cot_send(op):
        go(op, cott.at[zh], cott.at[zh], cs.at[0], cr.at[0], to_far)

    def forward_tile(k):
        def move(i, _):
            work[i] = gath[k, i]
            return 0
        lax.fori_loop(0, 64, move, 0, unroll=4)

        def slot(s, acc):
            prod = lax.dot_general(
                work[idx[CF + s]], adj[idx[PF + s]], (((1,), (1,)), ((), ())),
                preferred_element_type=F32,
            )
            acc = acc * idx[KF + s].astype(F32) + prod
            buf[s] = acc.astype(BF)
            return acc
        lax.fori_loop(0, NB, slot, jnp.zeros((CH, BS), F32), unroll=8)

        def pick(i, _):
            last = idx[LF + i]
            on = (jnp.minimum(last, 0) + 1).astype(F32)
            part[k, i] = (buf[jnp.maximum(last, 0)].astype(F32) * on).astype(BF)
            return 0
        lax.fori_loop(0, 16, pick, 0, unroll=4)

    z_own("start", 0)
    x_send("start", 0, z)

    for b in range(4):
        cott[zh, b] = cot[b * BS:(b + 1) * BS, :].astype(F32).T.astype(BF)
    z_stage("start", 0)
    cot_send("start")
    for i in range(2):
        for j in range(4):
            cols = pl.ds(pl.multiple_of((i * 2 + core) * FS, FS), FS)
            wt[i, :, j * FS:(j + 1) * FS] = weight[j * FS:(j + 1) * FS, cols].astype(F32).T.astype(BF)
    adj_copy.wait()

    def forward_step(k, _):
        @pl.when(k + 1 < K)
        def _():
            z_own("start", k + 1)
        x_pass("start", k)

        @pl.when(k + 1 < K)
        def _():
            x_send("start", k + 1, z)
            z_stage("start", k + 1)
        x_last(k)
        forward_tile(k)
        y_send("start", k)

        @pl.when(k > 0)
        def _():
            y_sum(k - 1)
            d_send("start", k - 1)

        @pl.when(k > 1)
        def _():
            d_pass("start", k - 2)
        return 0
    lax.fori_loop(0, K, forward_step, 0)
    y_sum(K - 1)
    d_send("start", K - 1)
    d_pass("start", K - 2)
    d_pass("start", K - 1)
    go("recv", cott.at[1 - zh], cott.at[1 - zh], cs.at[0], cr.at[0], to_far)
    for k in range(K):
        d_last(k)

    def mix_rows(b, dd):
        return gmix.at[b, pl.ds(pl.multiple_of(dd * FS, FS), FS), :]

    def mix_send(op, b):
        go(op, mix_rows(b, d), mix_rows(b, d), gs.at[b, 0], gr.at[b, 0], to_core)
        go(op, mix_rows(b, d_far), mix_rows(b, d_far), gs.at[b, 1], gr.at[b, 1], to_core)

    def mix_last(b):
        go("recv", mix_rows(b, d_core), mix_rows(b, d_core), gs.at[b, 0], gr.at[b, 0], to_core)
        go("recv", mix_rows(b, d_diag), mix_rows(b, d_diag), gs.at[b, 1], gr.at[b, 1], to_core)

    def dense(b, _):
        for own in (True, False):
            at = zh if own else 1 - zh
            dd = at * 2 + core
            m = jnp.dot(wt[at], agg[b], preferred_element_type=F32)
            sq = m * m
            t = jnp.tanh(GC * (m + 0.044715 * (sq * m)))
            half = 0.5 + 0.5 * t
            if own:
                actt[b] = (m * half).astype(BF)
            slope = half + 0.5 * m * (1.0 - t * t) * (GC + (3 * 0.044715 * GC) * sq)
            gmix[b, pl.ds(pl.multiple_of(dd * FS, FS), FS), :] = (
                cott[at, b].astype(F32) * slope
            ).astype(BF)
        mix_send("start", b)
        return 0
    lax.fori_loop(0, 4, dense, 0)

    def back_mix(b, _):
        mix_last(b)
        ga = jnp.dot(
            weight[pl.ds(pl.multiple_of(d * FS, FS), FS), :], gmix[b], preferred_element_type=F32
        ).astype(BF)
        for k in range(K):
            tgt[k, c * 4 + b] = ga[k * CH:(k + 1) * CH]
        return 0
    lax.fori_loop(0, 4, back_mix, 0)

    def t_send(op, k):
        own = tgt.at[k, pl.ds(c * 4, 4)]
        for o in range(1, 4):
            go(op, own, own, ts.at[k, o], tr.at[k, c], {"col": (c + o) % 4})

    def t_last(k):
        for o in range(1, 4):
            src = (c + o) % 4
            ref = tgt.at[k, pl.ds(src * 4, 4)]
            go("recv", ref, ref, ts.at[k, o], tr.at[k, src], {"col": src})

    for k in range(K):
        t_send("start", k)

    def gw_block(b, _):
        own = agg[b, pl.ds(pl.multiple_of(d * FS, FS), FS), :]
        for j in range(2):
            add = lax.dot_general(
                own, gmix[b, j * 256:(j + 1) * 256, :], (((1,), (1,)), ((), ())),
                preferred_element_type=F32,
            )
            for q in range(4):
                gw[q, :, j * 256:(j + 1) * 256] += add[q * 32:(q + 1) * 32]
        return 0
    gw[...] = jnp.zeros_like(gw)
    lax.fori_loop(0, 4, gw_block, 0)

    def wy(op, o):
        to = (c + o) % 4
        go(op, gw.at[to], gwy.at[c], wys.at[o], wyr.at[c], {"col": to})

    def wx(op, o):
        to = (x + o) % 4
        go(op, gwx.at[to], gwxr.at[x], wxs.at[o], wxr.at[x], {"row": to * 4 + z})

    def wz(op, o):
        go(op, gwz.at[z], gwz.at[z], wzs.at[o], wzr.at[z], {"row": x * 4 + (z + o) % 4})

    def vx(op, o):
        go(op, gwxa.at[x], gwxa.at[x], vxs.at[o], vxr.at[x], {"row": (x + o) % 4 * 4 + z})

    def vy(op, o):
        own = gw_out.at[pl.ds(pl.multiple_of(c * 32, 32), 32), :]
        go(op, own, own, vys.at[o], vyr.at[c], {"col": (c + o) % 4})

    def all3(fn, op):
        for o in range(1, 4):
            fn(op, o)

    def weight_step(it):
        @pl.when(it == 1)
        def _():
            for o in range(1, 4):
                src = (c + o) % 4
                go("recv", gw.at[c], gwy.at[src], wys.at[o], wyr.at[src], {"col": src})
            total = gw[c]
            for o in range(1, 4):
                total = total + gwy[(c + o) % 4]
            for q in range(4):
                gwx[q] = total[q * 8:(q + 1) * 8]
            all3(wx, "start")

        @pl.when(it == 2)
        def _():
            for o in range(1, 4):
                src = (x + o) % 4
                go("recv", gwx.at[x], gwxr.at[src], wxs.at[o], wxr.at[src], right)
            total = gwx[x]
            for o in range(1, 4):
                total = total + gwxr[(x + o) % 4]
            gwz[z] = total
            all3(wz, "start")

        @pl.when(it == 3)
        def _():
            for o in range(1, 4):
                src = (z + o) % 4
                go("recv", gwz.at[src], gwz.at[src], wzs.at[o], wzr.at[src], up)
            gwxa[x] = (gwz[0] + gwz[1]) + (gwz[2] + gwz[3])
            all3(vx, "start")

        @pl.when(it == 4)
        def _():
            for o in range(1, 4):
                src = (x + o) % 4
                go("recv", gwxa.at[src], gwxa.at[src], vxs.at[o], vxr.at[src], right)
            for q in range(4):
                gw_out[pl.ds(pl.multiple_of(c * 32 + q * 8, 8), 8), :] = gwxa[q]
            all3(vy, "start")

    all3(wy, "start")

    for b in range(4):
        act_out[b * BS:(b + 1) * BS, :] = actt[b].astype(F32).T.astype(BF)

    def backward_tile(k):
        t_last(k)

        def move(i, _):
            work[i] = tgt[k, i]
            return 0
        lax.fori_loop(0, 16, move, 0, unroll=4)

        def slot(s, acc):
            prod = jnp.dot(work[idx[RB + s]], adj[idx[PB + s]], preferred_element_type=F32)
            acc = acc * idx[KB + s].astype(F32) + prod
            buf[s] = acc.astype(BF)
            return acc
        lax.fori_loop(0, NB, slot, jnp.zeros((CH, BS), F32), unroll=8)

        def pick(i, _):
            last = idx[LB + i]
            on = (jnp.minimum(last, 0) + 1).astype(F32)
            terms[k, i] = (buf[jnp.maximum(last, 0)].astype(F32) * on).astype(BF)
            return 0
        lax.fori_loop(0, 64, pick, 0, unroll=4)

    def term(k, xx, zz, n=4, lo=0):
        return terms.at[k, pl.ds((xx * 4 + zz) * 4 + lo, n)]

    def far_half(op, k):
        def one(i, _):
            zz = (z + i) % 4
            go(op, term(k, xop, zz, 2), xol.at[k, zz], asr.at[k, zz], arl.at[k, zz], right)
            go(op, term(k, xop, zz, 2, 2), xor_.at[k, zz], asl.at[k, zz], arr.at[k, zz], left)
            return 0
        lax.fori_loop(0, 4, one, 0)

    def near_full(op, k):
        def one(i, _):
            zz = (z + i) % 4
            if op == "start":
                go("recv", term(k, xop, zz, 2), xol.at[k, zz], asr.at[k, zz], arl.at[k, zz], right)
                at = (xr1 * 4 + zz) * 4
                for h in range(2):
                    terms[k, at + h] = (terms[k, at + h].astype(F32) + xol[k, zz, h].astype(F32)).astype(BF)
            go(op, term(k, xr1, zz), xfl.at[k, zz], bsr.at[k, zz], brl.at[k, zz], right)
            if op == "start":
                go("recv", term(k, xop, zz, 2, 2), xor_.at[k, zz], asl.at[k, zz], arr.at[k, zz], left)
                at = (xl1 * 4 + zz) * 4 + 2
                for h in range(2):
                    terms[k, at + h] = (terms[k, at + h].astype(F32) + xor_[k, zz, h].astype(F32)).astype(BF)
            go(op, term(k, xl1, zz), xfr.at[k, zz], bsl.at[k, zz], brr.at[k, zz], left)
            return 0
        lax.fori_loop(0, 4, one, 0)

    def x_sum(k):
        def one(i, _):
            zz = (z + i) % 4
            go("recv", term(k, xr1, zz), xfl.at[k, zz], bsr.at[k, zz], brl.at[k, zz], right)
            go("recv", term(k, xl1, zz), xfr.at[k, zz], bsl.at[k, zz], brr.at[k, zz], left)
            for b in range(4):
                lines[k, zz, b] = (
                    terms[k, (x * 4 + zz) * 4 + b].astype(F32)
                    + xfl[k, zz, b].astype(F32)
                    + xfr[k, zz, b].astype(F32)
                ).astype(BF)
            return 0
        lax.fori_loop(0, 4, one, 0)

    def line_up(op, k):
        for zz in (3, 2, 1):
            @pl.when(z < zz)
            def _():
                if op == "start":
                    @pl.when(z > 0)
                    def _():
                        go("recv", lines.at[k, zz], zfd.at[k, zz], us.at[k, zz], dnr.at[k, zz], up)
                        for b in range(4):
                            lines[k, zz, b] = (
                                lines[k, zz, b].astype(F32) + zfd[k, zz, b].astype(F32)
                            ).astype(BF)
                go(op, lines.at[k, zz], zfd.at[k, zz], us.at[k, zz], dnr.at[k, zz], up)

    def line_down(op, k):
        for zz in (0, 1, 2):
            @pl.when(z > zz)
            def _():
                if op == "start":
                    @pl.when(z < 3)
                    def _():
                        go("recv", lines.at[k, zz], zfu.at[k, zz], dns.at[k, zz], ur.at[k, zz], down)
                        for b in range(4):
                            lines[k, zz, b] = (
                                lines[k, zz, b].astype(F32) + zfu[k, zz, b].astype(F32)
                            ).astype(BF)
                go(op, lines.at[k, zz], zfu.at[k, zz], dns.at[k, zz], ur.at[k, zz], down)

    def finish(k):
        rows = pl.ds(pl.multiple_of(k * CH, CH), CH)
        for b in range(4):
            fin[b, rows, :] = lines[k, z, b].astype(F32)

        @pl.when(z > 0)
        def _():
            go("recv", lines.at[k, z], zfd.at[k, z], us.at[k, z], dnr.at[k, z], up)
            for b in range(4):
                fin[b, rows, :] += zfd[k, z, b].astype(F32)

        @pl.when(z < 3)
        def _():
            go("recv", lines.at[k, z], zfu.at[k, z], dns.at[k, z], ur.at[k, z], down)
            for b in range(4):
                fin[b, rows, :] += zfu[k, z, b].astype(F32)

    def backward_step(it, _):
        @pl.when(it < K)
        def _():
            backward_tile(it)
            far_half("start", it)

        @pl.when((it > 0) & (it <= K))
        def _():
            x_sum(it - 1)

        @pl.when(it < K)
        def _():
            near_full("start", it)
        ku = it - 1 - z

        @pl.when((ku >= 0) & (ku < K))
        def _():
            line_up("start", ku)
        kd = it - 4 + z

        @pl.when((kd >= 0) & (kd < K))
        def _():
            line_down("start", kd)

        @pl.when(it >= 4)
        def _():
            finish(it - 4)
        weight_step(it)
        return 0
    lax.fori_loop(0, K + 4, backward_step, 0)

    for b in range(4):
        gf_out[b * BS:(b + 1) * BS, :] = fin[b].T.astype(BF)
    for o in range(1, 4):
        src = (c + o) % 4
        ref = gw_out.at[pl.ds(pl.multiple_of(src * 32, 32), 32), :]
        go("recv", ref, ref, vys.at[o], vyr.at[src], {"col": src})

    def drain(k, _):
        z_own("sent", k)
        x_send("sent", k, z)
        z_stage("sent", k)
        x_pass("sent", k)
        y_send("sent", k)
        d_send("sent", k)
        d_pass("sent", k)
        mix_send("sent", k)
        t_send("sent", k)
        far_half("sent", k)
        near_full("sent", k)
        line_up("sent", k)
        line_down("sent", k)
        return 0
    lax.fori_loop(0, K, drain, 0)
    cot_send("sent")
    for fn in (wy, wx, wz, vx, vy):
        all3(fn, "sent")


def layer(features, weight, cotangent, adjacency_blocks, block_rows, block_cols, tile_counts):
    blocks = adjacency_blocks[0, 0]
    rows_of, cols_of, count = block_rows[0, 0], block_cols[0, 0], tile_counts[0, 0]
    valid = jnp.arange(NB) < count
    idx = jnp.concatenate(
        sorted_slots(rows_of, cols_of, 64, valid, 16) + sorted_slots(cols_of, rows_of, 16, valid, 64)
    )
    vm = pl.BlockSpec(memory_space=pltpu.VMEM)
    dma = lambda *s: pltpu.SemaphoreType.DMA(s)
    per_chunk = (K, 4)
    scratch = [
        pltpu.VMEM((NB, BS, BS), BF),
        pltpu.VMEM((K, 64, CH, BS), BF),
        pltpu.VMEM((64, CH, BS), BF),
        pltpu.VMEM((NB, CH, BS), BF),
        pltpu.VMEM((K, 16, CH, BS), BF),
        pltpu.VMEM((K, 4, 4, CH, BS), BF),
        pltpu.VMEM((4, 512, BS), BF),
        pltpu.VMEM((2, 4, FS, BS), BF),
        pltpu.VMEM((4, 512, BS), BF),
        pltpu.VMEM((2, FS, 512), BF),
        pltpu.VMEM((4, FS, BS), BF),
        pltpu.VMEM((K, 16, CH, BS), BF),
        pltpu.VMEM((K, 64, CH, BS), BF),
        pltpu.VMEM((K, 4, 4, CH, BS), BF),
        pltpu.VMEM((K, 4, 4, CH, BS), BF),
        pltpu.VMEM((K, 4, 2, CH, BS), BF),
        pltpu.VMEM((K, 4, 2, CH, BS), BF),
        pltpu.VMEM((K, 4, 4, CH, BS), BF),
        pltpu.VMEM((K, 4, 4, CH, BS), BF),
        pltpu.VMEM((K, 4, 4, CH, BS), BF),
        pltpu.VMEM((4, FS, BS), F32),
        pltpu.VMEM((4, 32, 512), F32),
        pltpu.VMEM((4, 32, 512), F32),
        pltpu.VMEM((4, 8, 512), F32),
        pltpu.VMEM((4, 8, 512), F32),
        pltpu.VMEM((4, 8, 512), F32),
        pltpu.VMEM((4, 8, 512), F32),
        pltpu.SemaphoreType.DMA,
    ]
    scratch += [dma(*per_chunk) for _ in range(11)]
    scratch += [dma(K, 4), dma(K, 4), dma(K, 3), dma(K, 3), dma(1), dma(1), dma(4, 2), dma(4, 2), dma(K, 4), dma(K, 4)]
    scratch += [dma(*per_chunk) for _ in range(12)]
    scratch += [dma(4) for _ in range(10)]
    return pl.pallas_call(
        kernel,
        out_shape=(
            jax.ShapeDtypeStruct(features.shape, BF),
            jax.ShapeDtypeStruct(features.shape, BF),
            jax.ShapeDtypeStruct((FS, 512), F32),
        ),
        in_specs=[pl.BlockSpec(memory_space=pltpu.SMEM), vm, vm, vm, pl.BlockSpec(memory_space=pl.ANY)],
        out_specs=(vm, vm, vm),
        scratch_shapes=scratch,
        compiler_params=pltpu.CompilerParams(
            collective_id=0, has_side_effects=True, vmem_limit_bytes=56 << 20
        ),
        cost_estimate=pl.CostEstimate(flops=4_000_000_000, bytes_accessed=13_000_000, transcendentals=300_000),
    )(idx, features, weight, cotangent, blocks)


def solution(mesh):
    in_specs = (
        P(("row", "col"), "depth"),
        P(),
        P(("row", "col"), "depth"),
        P("row", "col", None, None, None),
        P("row", "col", None),
        P("row", "col", None),
        P("row", "col"),
    )
    out_specs = (P(("row", "col"), "depth"), P(("row", "col"), "depth"), P("depth", None))
    return jax.shard_map(layer, mesh=mesh, in_specs=in_specs, out_specs=out_specs, check_vma=False)
```

time: 1040 us -> 170 us (0.16)
  waiting for transfers between devices: 951 us -> 0 us
  Pallas kernels: 0 us -> 157 us
  local copies, waits for them, and re-layouts: 41.9 us -> 5.68 us
  matrix products: 31.7 us -> 0 us
  between operations: 14.9 us -> 1.31 us
    psum x1 -> x0, waiting for transfers between devices: 624 us -> none  [on_device(): grad_weight = lax.psum(weight_part, ('row', 'col'))]
    pallas_call x0 -> x1, Pallas kernels: none -> 157 us  [layer(): pl.pallas_call(kernel, out_shape=(jax.ShapeDtypeStruct(features.shape, BF...]
    all_gather x3 -> x0, waiting for transfers between devices: 153 us -> none  [the longest x1 105 us: on_device(): gathered = lax.all_gather(features, 'row', axis=0, tiled=True)]
    reduce_scatter x2 -> x0, waiting for transfers between devices: 126 us -> none  [the longest x1 105 us: on_device(): lax.psum_scatter(terms_back.astype(jnp.bfloat16), 'row', scatter_dimensio...]
    unnamed x8 -> x0, waiting for transfers between devices: 48 us -> none
    dot_general x7 -> x0, matrix products: 31.7 us -> none  [the longest x1 9.76 us: on_device(): jnp.einsum('nij,nif->njf', blocks, picked_back, preferred_element_type=jn...]
    dot_general x2 -> x0, local copies, waits for them, and re-layouts: 17.1 us -> none  [the longest x1 8.57 us: on_device(): jnp.einsum('nij,nif->njf', blocks, picked_back, preferred_element_type=jn...]
    gather x2 -> x0, local copies, waits for them, and re-layouts: 14.7 us -> none  [the longest x1 7.83 us: on_device(): picked = source[cols_of]]
  transfers between devices with their start and end apart: 7 -> 0, of which waited for: 7 -> 0; matrix products, arithmetic and copies ran while one was open for 4% -> 0% of each run, Pallas kernels for 0% -> 0%
where the time goes in v1:
time: 170 us; the launch traced here: 169 us
  Pallas kernels  157 us (92%)
  local copies, waits for them, and re-layouts  5.68 us (3%)
  other arithmetic  5 us (3%)
    pallas_call x1, Pallas kernels, layer(): pl.pallas_call(kernel, out_shape=(jax.ShapeDtypeStruct(features.shape, BF...  157 us
    unnamed x3, local copies, waits for them, and re-layouts  5.01 us

profile of v1, /device:TPU:8, one launch (start us, length us, event | category | flops | bytes accessed | tf_op | source)
XLA Modules:
  0.0 168.8 jit_solution(16218331098302502353)
XLA Ops:
  1.3 0.8 fusion.1
  2.1 0.8 convert_reduce_fusion.3
  2.8 0.8 fusion.4
  3.6 0.8 convert_reduce_fusion.2
  4.4 0.7 fusion.6
  5.1 0.2 convert_reduce_fusion
  5.3 0.9 select_reduce_fusion
  6.2 0.1 compare_convert_fusion.1
  6.2 0.1 compare_convert_fusion
  6.3 0.7 concatenate.11.idx
  7.0 156.8 %shard_map.94 = (bf16[1024,128]{1,0:T(8,128)(2,1)}, bf16[1024,128]{1,0:T(8,128)(2,1)}, f32[128,512]{1,0:T(8,128)}) custom-call(s32[560]{0:T(1024)} %concatenate.11.idx, bf16[1024,128]{1,0:T(8,128)(2,1)} %feat.1, bf16[512,512]{1,0:T(8,128)(2,1)} %weight.1, bf16[1024,128]{1,0:T(8,128)(2,1)} %cot.1, bf16[80,256,256]{2,1,0:T(8,128)(2,1)} %bitcast.20), custom_call_target="tpu_custom_call" | custom-call | flops 4000000000 | bytes 13000000 | tf_op jit(solution)/shard_map/pallas_call | solution.py:625
  163.8 1.7 copy.14
  165.4 1.7 copy.15
  167.1 1.7 copy.16
  (3 shorter events, 0.0 us)

commit v2 on v1

v2 whole, which is shorter than its diff:
```python
import jax
import jax.numpy as jnp
from jax import lax
from jax.experimental import pallas as pl
from jax.experimental.pallas import tpu as pltpu
from jax.sharding import PartitionSpec as P

BF = jnp.bfloat16
F32 = jnp.float32
K = 2
CH = 64
BS = 256
PB = 1
NP = 4 // PB
FS = 128
GC = 0.7978845608028654
NB = 80
PF, CF, KF, LF, QB, RB, KB, LB = range(8)


def slot_order(major, minor, span, valid):
    side = major.shape[0]
    lane = lax.broadcasted_iota(jnp.int32, (side, side), 1)
    key = jnp.where(valid, major * span + minor, 4096 + lane)
    key_t, major_t, minor_t = key.T, major.T, minor.T
    valid_t = valid.astype(jnp.int32).T > 0
    rank = jnp.sum((key < key_t).astype(jnp.int32), axis=1, keepdims=True)
    at = lax.broadcasted_iota(jnp.int32, (side, side), 0)

    def pick(cond, value):
        return jnp.sum(jnp.where(cond, value, 0), axis=0, keepdims=True)

    hit = rank == lane
    perm = pick(hit, at)
    minor_sorted = pick(hit, minor_t)
    major_sorted = pick(hit, major_t + 1)
    before = pick(rank + 1 == lane, major_t + 1)
    keep = (major_sorted == before).astype(jnp.int32)
    ends = pick(valid_t & (major_t <= lane), 1)
    used = pick(valid_t & (major_t == lane), 1)
    last = jnp.where(used > 0, ends - 1, -1)
    return [perm, minor_sorted, keep, last]


def kernel(
    count, rows_of, cols_of, feat, weight, cot, adj_hbm,
    act_out, gf_out, gw_out,
    idx, table, idx_sem,
    adj, gath, work, buf, part, yrecv, agg, cott, gmix, wt,
    tgt, terms, xfl, xfr, xol, xor_, lines, zfd, zfu, z3d, z3u, xo3, xf3,
    gw, gwy, gwx, gwxr, gwz, gwxa,
    adj_sem,
    zsu, zsd, zr, xsr, xsl, xrl, xrr, osr, osl, orl, orr,
    ys, yr, ds, dr, cs, cr, gs, gr, ts, tr,
    asr, asl, arl, arr, bsr, bsl, brl, brr, us, dns, ur, dnr,
    u3s, d3s, u3r, d3r, o3s, o3r, f3s, f3r,
    wys, wyr, wxs, wxr, wzs, wzr, vxs, vxr, vys, vyr,
):
    row = lax.axis_index("row")
    c = lax.axis_index("col")
    d = lax.axis_index("depth")
    x, z = row // 4, row % 4
    zh, core = d // 2, d % 2
    right = {"row": (x + 1) % 4 * 4 + z}
    left = {"row": (x + 3) % 4 * 4 + z}
    up = {"row": x * 4 + (z + 1) % 4}
    down = {"row": x * 4 + (z + 3) % 4}
    d_core = zh * 2 + (1 - core)
    d_far = (1 - zh) * 2 + core
    d_diag = (1 - zh) * 2 + (1 - core)
    to_core = {"depth": d_core}
    to_far = {"depth": d_far}
    xr1, xl1, xop = (x + 1) % 4, (x + 3) % 4, (x + 2) % 4

    def rcopy(src, dst, ssem, rsem, dev):
        return pltpu.make_async_remote_copy(
            src_ref=src, dst_ref=dst, send_sem=ssem, recv_sem=rsem,
            device_id=dev, device_id_type=pl.DeviceIdType.MESH,
        )

    def go(op, *args):
        copy = rcopy(*args)
        if op == "start":
            copy.start()
        elif op == "sent":
            copy.wait_send()
        else:
            copy.wait_recv()

    barrier = pltpu.get_barrier_semaphore()
    for o in range(1, 4):
        for dev in (
            {"row": (x + o) % 4 * 4 + z},
            {"row": x * 4 + (z + o) % 4},
            {"col": (c + o) % 4},
        ):
            pl.semaphore_signal(barrier, inc=1, device_id=dev, device_id_type=pl.DeviceIdType.MESH)
    for dev in (to_core, to_far):
        pl.semaphore_signal(barrier, inc=1, device_id=dev, device_id_type=pl.DeviceIdType.MESH)

    adj_copy = pltpu.make_async_copy(adj_hbm, adj, adj_sem)
    adj_copy.start()

    for b in range(4):
        flip = feat[b * BS:(b + 1) * BS, :].astype(F32).T.astype(BF)
        for k in range(K):
            gath[k, row * 4 + b] = flip[k * CH:(k + 1) * CH]

    pl.semaphore_wait(barrier, 11)

    def shard(k, xx, zz):
        return gath.at[k, pl.ds((xx * 4 + zz) * 4, 4)]

    def lower(k, xx, zz):
        return gath.at[k, pl.ds((xx * 4 + zz) * 4, 2)]

    def upper(k, xx, zz):
        return gath.at[k, pl.ds((xx * 4 + zz) * 4 + 2, 2)]

    def z_up(op, k, zz):
        go(op, shard(k, x, zz), shard(k, x, zz), zsu.at[k, zz], zr.at[k, zz], up)

    def z_down(op, k, zz):
        go(op, shard(k, x, zz), shard(k, x, zz), zsd.at[k, zz], zr.at[k, zz], down)

    def z_own(op, k):
        @pl.when(z < 3)
        def _():
            z_up(op, k, z)

        @pl.when(z > 0)
        def _():
            z_down(op, k, z)

    def x_send(op, k, zz):
        go(op, shard(k, x, zz), shard(k, x, zz), xsr.at[k, zz], xrl.at[k, zz], right)
        go(op, shard(k, x, zz), shard(k, x, zz), xsl.at[k, zz], xrr.at[k, zz], left)

    def z_stage(op, k):
        for o in range(1, 4):
            @pl.when(z >= o)
            def _():
                zz = z - o
                if op == "start":
                    z_up("recv", k, zz)

                @pl.when(z < 3)
                def _():
                    z_up(op, k, zz)
                x_send(op, k, zz)

            @pl.when(z + o <= 3)
            def _():
                zz = z + o
                if op == "start":
                    z_down("recv", k, zz)

                @pl.when(z > 0)
                def _():
                    z_down(op, k, zz)
                x_send(op, k, zz)

    def x_pass(op, k):
        def one(i, _):
            zz = (z + i) % 4
            if op == "start":
                go("recv", shard(k, xl1, zz), shard(k, xl1, zz), xsr.at[k, zz], xrl.at[k, zz], right)
            go(op, lower(k, xl1, zz), lower(k, xl1, zz), osr.at[k, zz], orl.at[k, zz], right)
            if op == "start":
                go("recv", shard(k, xr1, zz), shard(k, xr1, zz), xsl.at[k, zz], xrr.at[k, zz], left)
            go(op, upper(k, xr1, zz), upper(k, xr1, zz), osl.at[k, zz], orr.at[k, zz], left)
            return 0
        lax.fori_loop(0, 4, one, 0)

    def x_last(k):
        def one(i, _):
            zz = (z + i) % 4
            go("recv", lower(k, xop, zz), lower(k, xop, zz), osr.at[k, zz], orl.at[k, zz], right)
            go("recv", upper(k, xop, zz), upper(k, xop, zz), osl.at[k, zz], orr.at[k, zz], left)
            return 0
        lax.fori_loop(0, 4, one, 0)

    def y_send(op, k, p):
        for o in range(1, 4):
            to = (c + o) % 4
            go(
                op, part.at[k, pl.ds(to * 4 + p * PB, PB)], yrecv.at[k, c, pl.ds(p * PB, PB)],
                ys.at[k, p, o], yr.at[k, p, c], {"col": to},
            )

    def y_sum(k, p):
        for o in range(1, 4):
            src = (c + o) % 4
            go(
                "recv", part.at[k, pl.ds(c * 4 + p * PB, PB)], yrecv.at[k, src, pl.ds(p * PB, PB)],
                ys.at[k, p, o], yr.at[k, p, src], {"col": src},
            )
        for q in range(PB):
            b = p * PB + q
            total = part[k, c * 4 + b].astype(F32)
            for o in range(1, 4):
                total = total + yrecv[k, (c + o) % 4, b].astype(F32)
            agg[b, pl.ds(pl.multiple_of(d * FS + k * CH, CH), CH), :] = total.astype(BF)

    def agg_rows(dd, k, p):
        return agg.at[pl.ds(p * PB, PB), pl.ds(pl.multiple_of(dd * FS + k * CH, CH), CH), :]

    def d_send(op, k, p):
        own = agg_rows(d, k, p)
        go(op, own, own, ds.at[k, p, 1], dr.at[k, p, 1], to_far)
        go(op, own, own, ds.at[k, p, 0], dr.at[k, p, 0], to_core)

    def d_pass(op, k, p):
        far = agg_rows(d_far, k, p)
        if op == "start":
            go("recv", far, far, ds.at[k, p, 1], dr.at[k, p, 1], to_far)
        go(op, far, far, ds.at[k, p, 2], dr.at[k, p, 2], to_core)

    def d_last(k, p):
        near, diag = agg_rows(d_core, k, p), agg_rows(d_diag, k, p)
        go("recv", near, near, ds.at[k, p, 0], dr.at[k, p, 0], to_core)
        go("recv", diag, diag, ds.at[k, p, 2], dr.at[k, p, 2], to_core)

    def blocks(fn, *args):
        def one(p, _):
            fn(*args, p)
            return 0
        lax.fori_loop(0, NP, one, 0)

    def cot_send(op):
        go(op, cott.at[zh], cott.at[zh], cs.at[0], cr.at[0], to_far)

    def forward_tile(k):
        def move(i, _):
            work[i] = gath[k, i]
            return 0
        lax.fori_loop(0, 64, move, 0, unroll=4)

        def slot(s, acc):
            prod = lax.dot_general(
                work[idx[CF, s]], adj[idx[PF, s]], (((1,), (1,)), ((), ())),
                preferred_element_type=F32,
            )
            acc = acc * idx[KF, s].astype(F32) + prod
            buf[s] = acc.astype(BF)
            return acc
        lax.fori_loop(0, NB, slot, jnp.zeros((CH, BS), F32), unroll=8)

        def pick(p, _):
            for q in range(4):
                for e in range(PB):
                    i = q * 4 + p * PB + e
                    last = idx[LF, i]
                    on = (jnp.minimum(last, 0) + 1).astype(F32)
                    part[k, i] = (buf[jnp.maximum(last, 0)].astype(F32) * on).astype(BF)
            y_send("start", k, p)
            return 0
        lax.fori_loop(0, NP, pick, 0)

    for k in range(min(2, K)):
        z_own("start", k)
        x_send("start", k, z)

    table[0:2, :] = jnp.zeros((2, 128), jnp.int32)
    table[0:1, 0:NB] = rows_of[...]
    table[1:2, 0:NB] = cols_of[...]
    rows_all = jnp.broadcast_to(table[0:1, :], (128, 128))
    cols_all = jnp.broadcast_to(table[1:2, :], (128, 128))
    valid = lax.broadcasted_iota(jnp.int32, (128, 128), 1) < count[0, 0]
    order = slot_order(rows_all, cols_all, 64, valid) + slot_order(cols_all, rows_all, 16, valid)
    for i in range(8):
        table[i:i + 1, :] = order[i]
    idx_copy = pltpu.make_async_copy(table, idx, idx_sem)
    idx_copy.start()

    z_stage("start", 0)
    for b in range(4):
        cott[zh, b] = cot[b * BS:(b + 1) * BS, :].astype(F32).T.astype(BF)
    if K > 1:
        z_stage("start", 1)
    if K == 2:
        cot_send("start")
    for i in range(2):
        for j in range(4):
            cols = pl.ds(pl.multiple_of((i * 2 + core) * FS, FS), FS)
            wt[i, :, j * FS:(j + 1) * FS] = weight[j * FS:(j + 1) * FS, cols].astype(F32).T.astype(BF)
    x_pass("start", 0)
    idx_copy.wait()
    adj_copy.wait()

    def forward_step(k, _):
        @pl.when(k + 2 < K)
        def _():
            z_own("start", k + 2)
            x_send("start", k + 2, z)
            z_stage("start", k + 2)

        @pl.when(k + 3 == K)
        def _():
            cot_send("start")

        @pl.when(k + 1 < K)
        def _():
            x_pass("start", k + 1)

        @pl.when(k > 0)
        def _():
            def one(p, _):
                y_sum(k - 1, p)
                d_send("start", k - 1, p)
                return 0
            lax.fori_loop(0, NP, one, 0)
        x_last(k)

        forward_tile(k)

        @pl.when(k > 0)
        def _():
            blocks(d_pass, "start", k - 1)
        return 0
    lax.fori_loop(0, K, forward_step, 0)

    def last_sum(p, _):
        y_sum(K - 1, p)
        d_send("start", K - 1, p)
        return 0
    lax.fori_loop(0, NP, last_sum, 0)
    go("recv", cott.at[1 - zh], cott.at[1 - zh], cs.at[0], cr.at[0], to_far)

    def mix_rows(p, dd):
        return gmix.at[pl.ds(p * PB, PB), pl.ds(pl.multiple_of(dd * FS, FS), FS), :]

    def mix_send(op, p):
        go(op, mix_rows(p, d), mix_rows(p, d), gs.at[p, 0], gr.at[p, 0], to_core)
        go(op, mix_rows(p, d_far), mix_rows(p, d_far), gs.at[p, 1], gr.at[p, 1], to_core)

    def mix_last(p):
        go("recv", mix_rows(p, d_core), mix_rows(p, d_core), gs.at[p, 0], gr.at[p, 0], to_core)
        go("recv", mix_rows(p, d_diag), mix_rows(p, d_diag), gs.at[p, 1], gr.at[p, 1], to_core)

    def dense(b):
        for own in (True, False):
            at = zh if own else 1 - zh
            dd = at * 2 + core
            m = jnp.dot(wt[at], agg[b], preferred_element_type=F32)
            sq = m * m
            t = jnp.tanh(GC * (m + 0.044715 * (sq * m)))
            half = 0.5 + 0.5 * t
            if own:
                act_out[b] = (m * half).astype(BF)
            slope = half + 0.5 * m * (1.0 - t * t) * (GC + (3 * 0.044715 * GC) * sq)
            gmix[b, pl.ds(pl.multiple_of(dd * FS, FS), FS), :] = (
                cott[at, b].astype(F32) * slope
            ).astype(BF)

    def back_mix(p):
        mix_last(p)

        def one(q, _):
            b = p * PB + q
            ga = jnp.dot(
                weight[pl.ds(pl.multiple_of(d * FS, FS), FS), :], gmix[b], preferred_element_type=F32
            ).astype(BF)
            for k in range(K):
                tgt[k, c * 4 + b] = ga[k * CH:(k + 1) * CH]
            return 0
        lax.fori_loop(0, PB, one, 0)
        t_send("start", 0, p)

    def t_send(op, k, p):
        own = tgt.at[k, pl.ds(c * 4 + p * PB, PB)]
        for o in range(1, 4):
            go(op, own, own, ts.at[k, p, o], tr.at[k, p, c], {"col": (c + o) % 4})

    def t_last(k):
        def one(p, _):
            for o in range(1, 4):
                src = (c + o) % 4
                ref = tgt.at[k, pl.ds(src * 4 + p * PB, PB)]
                go("recv", ref, ref, ts.at[k, p, o], tr.at[k, p, src], {"col": src})
            return 0
        lax.fori_loop(0, NP, one, 0)

    d_pass("start", K - 1, 0)

    def middle(p, _):
        @pl.when(p < NP - 1)
        def _():
            d_pass("start", K - 1, p + 1)
        for k in range(K):
            d_last(k, p)

        def one(q, _):
            dense(p * PB + q)
            return 0
        lax.fori_loop(0, PB, one, 0)
        mix_send("start", p)

        @pl.when(p > 0)
        def _():
            back_mix(p - 1)
        return 0
    lax.fori_loop(0, NP, middle, 0)
    back_mix(NP - 1)
    for k in range(1, K):
        blocks(t_send, "start", k)

    def gw_block(b, _):
        own = agg[b, pl.ds(pl.multiple_of(d * FS, FS), FS), :]
        for j in range(2):
            add = lax.dot_general(
                own, gmix[b, j * 256:(j + 1) * 256, :], (((1,), (1,)), ((), ())),
                preferred_element_type=F32,
            )
            for q in range(4):
                gw[q, :, j * 256:(j + 1) * 256] += add[q * 32:(q + 1) * 32]
        return 0
    gw[...] = jnp.zeros_like(gw)
    lax.fori_loop(0, 4, gw_block, 0)

    def wy(op, o):
        to = (c + o) % 4
        go(op, gw.at[to], gwy.at[c], wys.at[o], wyr.at[c], {"col": to})

    def wx(op, o):
        to = (x + o) % 4
        go(op, gwx.at[to], gwxr.at[x], wxs.at[o], wxr.at[x], {"row": to * 4 + z})

    def wz(op, o):
        go(op, gwz.at[z], gwz.at[z], wzs.at[o], wzr.at[z], {"row": x * 4 + (z + o) % 4})

    def vx(op, o):
        go(op, gwxa.at[x], gwxa.at[x], vxs.at[o], vxr.at[x], {"row": (x + o) % 4 * 4 + z})

    def vy(op, o):
        own = gw_out.at[pl.ds(pl.multiple_of(c * 32, 32), 32), :]
        go(op, own, own, vys.at[o], vyr.at[c], {"col": (c + o) % 4})

    def all3(fn, op):
        for o in range(1, 4):
            fn(op, o)

    def weight_step(it):
        if it == 1:
            for o in range(1, 4):
                src = (c + o) % 4
                go("recv", gw.at[c], gwy.at[src], wys.at[o], wyr.at[src], {"col": src})
            total = gw[c]
            for o in range(1, 4):
                total = total + gwy[(c + o) % 4]
            for q in range(4):
                gwx[q] = total[q * 8:(q + 1) * 8]
            all3(wx, "start")

        if it == 2:
            for o in range(1, 4):
                src = (x + o) % 4
                go("recv", gwx.at[x], gwxr.at[src], wxs.at[o], wxr.at[src], right)
            total = gwx[x]
            for o in range(1, 4):
                total = total + gwxr[(x + o) % 4]
            gwz[z] = total
            all3(wz, "start")

        if it == 3:
            for o in range(1, 4):
                src = (z + o) % 4
                go("recv", gwz.at[src], gwz.at[src], wzs.at[o], wzr.at[src], up)
            gwxa[x] = (gwz[0] + gwz[1]) + (gwz[2] + gwz[3])
            all3(vx, "start")

        if it == 4:
            for o in range(1, 4):
                src = (x + o) % 4
                go("recv", gwxa.at[src], gwxa.at[src], vxs.at[o], vxr.at[src], right)
            for q in range(4):
                gw_out[pl.ds(pl.multiple_of(c * 32 + q * 8, 8), 8), :] = gwxa[q]
            all3(vy, "start")

    all3(wy, "start")

    def backward_tile(k):
        t_last(k)

        def move(i, _):
            work[i] = tgt[k, i]
            return 0
        lax.fori_loop(0, 16, move, 0, unroll=4)

        def slot(s, acc):
            prod = jnp.dot(work[idx[RB, s]], adj[idx[QB, s]], preferred_element_type=F32)
            acc = acc * idx[KB, s].astype(F32) + prod
            buf[s] = acc.astype(BF)
            return acc
        lax.fori_loop(0, NB, slot, jnp.zeros((CH, BS), F32), unroll=8)

        def pick(i, _):
            last = idx[LB, i]
            on = (jnp.minimum(last, 0) + 1).astype(F32)
            terms[k, i // 16, i // 4 % 4, i % 4] = (buf[jnp.maximum(last, 0)].astype(F32) * on).astype(BF)
            return 0
        lax.fori_loop(0, 64, pick, 0, unroll=4)

    HALF = CH // 2
    order = (3, 0, 2, 1)

    def add_to(ref, at, got):
        ref[at] = (ref[at].astype(F32) + got.astype(F32)).astype(BF)

    def term(k, xx, zz, lo=0, n=CH):
        return terms.at[k, xx, zz, pl.ds(0, 3), pl.ds(lo, n)]

    def far_half(op, k):
        for zz in order:
            go(op, term(k, xop, zz, 0, HALF), xol.at[k, zz], asr.at[k, zz], arl.at[k, zz], right)
            go(op, term(k, xop, zz, HALF, HALF), xor_.at[k, zz], asl.at[k, zz], arr.at[k, zz], left)

    def near_full(op, k):
        for zz in order:
            if op == "start":
                go("recv", term(k, xop, zz, 0, HALF), xol.at[k, zz], asr.at[k, zz], arl.at[k, zz], right)
                for b in range(3):
                    add_to(terms, (k, xr1, zz, b, slice(0, HALF)), xol[k, zz, b])
            go(op, term(k, xr1, zz), xfl.at[k, zz], bsr.at[k, zz], brl.at[k, zz], right)
            if op == "start":
                go("recv", term(k, xop, zz, HALF, HALF), xor_.at[k, zz], asl.at[k, zz], arr.at[k, zz], left)
                for b in range(3):
                    add_to(terms, (k, xl1, zz, b, slice(HALF, CH)), xor_[k, zz, b])
            go(op, term(k, xl1, zz), xfr.at[k, zz], bsl.at[k, zz], brr.at[k, zz], left)

    def x_sum(k):
        for zz in order:
            go("recv", term(k, xr1, zz), xfl.at[k, zz], bsr.at[k, zz], brl.at[k, zz], right)
            go("recv", term(k, xl1, zz), xfr.at[k, zz], bsl.at[k, zz], brr.at[k, zz], left)
            for b in range(3):
                lines[k, zz, b] = (
                    terms[k, x, zz, b].astype(F32) + xfl[k, zz, b].astype(F32) + xfr[k, zz, b].astype(F32)
                ).astype(BF)
            if zz > 0:
                @pl.when(z == 0)
                def _():
                    up_msg("start", k, zz)
            if zz < 3:
                @pl.when(z == 3)
                def _():
                    down_msg("start", k, zz)

    def up_msg(op, k, zz):
        go(op, lines.at[k, zz], zfd.at[k, zz], us.at[k, zz], dnr.at[k, zz], up)

    def down_msg(op, k, zz):
        go(op, lines.at[k, zz], zfu.at[k, zz], dns.at[k, zz], ur.at[k, zz], down)

    def pass_on(op, k):
        for at, zz in ((1, 3), (1, 2), (2, 3)):
            @pl.when(z == at)
            def _():
                if op == "start":
                    up_msg("recv", k, zz)
                    for b in range(3):
                        add_to(lines, (k, zz, b), zfd[k, zz, b])
                up_msg(op, k, zz)

            @pl.when(z == 3 - at)
            def _():
                if op == "start":
                    down_msg("recv", k, 3 - zz)
                    for b in range(3):
                        add_to(lines, (k, 3 - zz, b), zfu[k, 3 - zz, b])
                down_msg(op, k, 3 - zz)

    def x_sum_sent(k):
        for zz in (1, 2, 3):
            @pl.when(z == 0)
            def _():
                up_msg("sent", k, zz)

            @pl.when(z == 3)
            def _():
                down_msg("sent", k, 3 - zz)

    def finish(k):
        rows = pl.ds(k * CH, CH)
        for b in range(3):
            gf_out[b, rows, :] = lines[k, z, b].astype(F32)

        @pl.when(z > 0)
        def _():
            up_msg("recv", k, z)
            for b in range(3):
                gf_out[b, rows, :] += zfd[k, z, b].astype(F32)

        @pl.when(z < 3)
        def _():
            down_msg("recv", k, z)
            for b in range(3):
                gf_out[b, rows, :] += zfu[k, z, b].astype(F32)

    def up3(op, k, zz):
        go(op, terms.at[k, :, zz, 3], z3d.at[k, zz], u3s.at[k, zz], d3r.at[k, zz], up)

    def down3(op, k, zz):
        go(op, terms.at[k, :, zz, 3], z3u.at[k, zz], d3s.at[k, zz], u3r.at[k, zz], down)

    def line3(op, k, stage):
        for zz in range(3, stage, -1):
            @pl.when(z == stage)
            def _():
                if op == "start" and stage > 0:
                    up3("recv", k, zz)
                    for q in range(4):
                        add_to(terms, (k, q, zz, 3), z3d[k, zz, q])
                up3(op, k, zz)

            @pl.when(z == 3 - stage)
            def _():
                if op == "start" and stage > 0:
                    down3("recv", k, 3 - zz)
                    for q in range(4):
                        add_to(terms, (k, q, 3 - zz, 3), z3u[k, 3 - zz, q])
                down3(op, k, 3 - zz)

    def line3_sum(k):
        @pl.when(z > 0)
        def _():
            up3("recv", k, z)
            for q in range(4):
                add_to(terms, (k, q, z, 3), z3d[k, z, q])

        @pl.when(z < 3)
        def _():
            down3("recv", k, z)
            for q in range(4):
                add_to(terms, (k, q, z, 3), z3u[k, z, q])

    def one3(k, xx, lo=0, n=CH):
        return terms.at[k, xx, z, 3, pl.ds(lo, n)]

    def far3(op, k):
        go(op, one3(k, xop, 0, HALF), xo3.at[k, 0], o3s.at[k, 0], o3r.at[k, 0], right)
        go(op, one3(k, xop, HALF, HALF), xo3.at[k, 1], o3s.at[k, 1], o3r.at[k, 1], left)

    def near3(op, k):
        if op == "start":
            go("recv", one3(k, xop, 0, HALF), xo3.at[k, 0], o3s.at[k, 0], o3r.at[k, 0], right)
            add_to(terms, (k, xr1, z, 3, slice(0, HALF)), xo3[k, 0])
        go(op, one3(k, xr1), xf3.at[k, 0], f3s.at[k, 0], f3r.at[k, 0], right)
        if op == "start":
            go("recv", one3(k, xop, HALF, HALF), xo3.at[k, 1], o3s.at[k, 1], o3r.at[k, 1], left)
            add_to(terms, (k, xl1, z, 3, slice(HALF, CH)), xo3[k, 1])
        go(op, one3(k, xl1), xf3.at[k, 1], f3s.at[k, 1], f3r.at[k, 1], left)

    def finish3(k):
        go("recv", one3(k, xr1), xf3.at[k, 0], f3s.at[k, 0], f3r.at[k, 0], right)
        go("recv", one3(k, xl1), xf3.at[k, 1], f3s.at[k, 1], f3r.at[k, 1], left)
        gf_out[3, k * CH:(k + 1) * CH, :] = (
            terms[k, x, z, 3].astype(F32) + xf3[k, 0].astype(F32) + xf3[k, 1].astype(F32)
        )

    backward_tile(0)
    far_half("start", 0)
    line3("start", 0, 0)
    backward_tile(1)
    line3("start", 1, 0)
    line3("start", 0, 1)
    near_full("start", 0)
    far_half("start", 1)
    line3("start", 0, 2)
    weight_step(1)
    line3("start", 1, 1)
    line3_sum(0)
    far3("start", 0)
    line3("start", 1, 2)
    x_sum(0)
    near_full("start", 1)
    near3("start", 0)
    line3_sum(1)
    far3("start", 1)
    weight_step(2)
    pass_on("start", 0)
    near3("start", 1)
    finish3(0)
    weight_step(3)
    finish(0)
    finish3(1)
    weight_step(4)
    x_sum(1)
    pass_on("start", 1)
    finish(1)

    for o in range(1, 4):
        src = (c + o) % 4
        ref = gw_out.at[pl.ds(pl.multiple_of(src * 32, 32), 32), :]
        go("recv", ref, ref, vys.at[o], vyr.at[src], {"col": src})

    def drain(k, _):
        z_own("sent", k)
        x_send("sent", k, z)
        z_stage("sent", k)
        x_pass("sent", k)
        for fn in (y_send, d_send, d_pass, t_send):
            blocks(fn, "sent", k)
        far_half("sent", k)
        near_full("sent", k)
        x_sum_sent(k)
        pass_on("sent", k)
        for stage in range(3):
            line3("sent", k, stage)
        far3("sent", k)
        near3("sent", k)
        return 0
    lax.fori_loop(0, K, drain, 0)
    blocks(mix_send, "sent")
    cot_send("sent")
    for fn in (wy, wx, wz, vx, vy):
        all3(fn, "sent")


def write_out(act_t, gf_t, gw, act, gf, gw_out):
    gw_out[...] = gw[...]
    for b in range(4):
        act[b * BS:(b + 1) * BS, :] = act_t[b].astype(F32).T.astype(BF)
        gf[b * BS:(b + 1) * BS, :] = gf_t[b].T.astype(BF)


def layer(features, weight, cotangent, adjacency_blocks, block_rows, block_cols, tile_counts):
    blocks = adjacency_blocks[0, 0]
    vm = pl.BlockSpec(memory_space=pltpu.VMEM)
    dma = lambda *s: pltpu.SemaphoreType.DMA(s)
    per_chunk = (K, 4)
    scratch = [
        pltpu.SMEM((8, 128), jnp.int32),
        pltpu.VMEM((8, 128), jnp.int32),
        pltpu.SemaphoreType.DMA,
        pltpu.VMEM((NB, BS, BS), BF),
        pltpu.VMEM((K, 64, CH, BS), BF),
        pltpu.VMEM((64, CH, BS), BF),
        pltpu.VMEM((NB, CH, BS), BF),
        pltpu.VMEM((K, 16, CH, BS), BF),
        pltpu.VMEM((K, 4, 4, CH, BS), BF),
        pltpu.VMEM((4, 512, BS), BF),
        pltpu.VMEM((2, 4, FS, BS), BF),
        pltpu.VMEM((4, 512, BS), BF),
        pltpu.VMEM((2, FS, 512), BF),
        pltpu.VMEM((K, 16, CH, BS), BF),
        pltpu.VMEM((K, 4, 4, 4, CH, BS), BF),
        pltpu.VMEM((K, 4, 3, CH, BS), BF),
        pltpu.VMEM((K, 4, 3, CH, BS), BF),
        pltpu.VMEM((K, 4, 3, CH // 2, BS), BF),
        pltpu.VMEM((K, 4, 3, CH // 2, BS), BF),
        pltpu.VMEM((K, 4, 3, CH, BS), BF),
        pltpu.VMEM((K, 4, 3, CH, BS), BF),
        pltpu.VMEM((K, 4, 3, CH, BS), BF),
        pltpu.VMEM((K, 4, 4, CH, BS), BF),
        pltpu.VMEM((K, 4, 4, CH, BS), BF),
        pltpu.VMEM((K, 2, CH // 2, BS), BF),
        pltpu.VMEM((K, 2, CH, BS), BF),
        pltpu.VMEM((4, 32, 512), F32),
        pltpu.VMEM((4, 32, 512), F32),
        pltpu.VMEM((4, 8, 512), F32),
        pltpu.VMEM((4, 8, 512), F32),
        pltpu.VMEM((4, 8, 512), F32),
        pltpu.VMEM((4, 8, 512), F32),
        pltpu.SemaphoreType.DMA,
    ]
    scratch += [dma(*per_chunk) for _ in range(11)]
    scratch += [dma(K, 4, 4), dma(K, 4, 4), dma(K, 4, 3), dma(K, 4, 3), dma(1), dma(1), dma(4, 2), dma(4, 2)]
    scratch += [dma(K, 4, 4), dma(K, 4, 4)]
    scratch += [dma(*per_chunk) for _ in range(16)] + [dma(K, 2) for _ in range(4)]
    scratch += [dma(4) for _ in range(10)]
    act_t, gf_t, grad_weight = pl.pallas_call(
        kernel,
        out_shape=(
            jax.ShapeDtypeStruct((4, FS, BS), BF),
            jax.ShapeDtypeStruct((4, FS, BS), F32),
            jax.ShapeDtypeStruct((FS, 512), F32),
        ),
        in_specs=[pl.BlockSpec(memory_space=pltpu.SMEM)] + [vm] * 5 + [pl.BlockSpec(memory_space=pl.ANY)],
        out_specs=(vm, vm, vm),
        scratch_shapes=scratch,
        compiler_params=pltpu.CompilerParams(
            collective_id=0, has_side_effects=True, vmem_limit_bytes=56 << 20
        ),
        cost_estimate=pl.CostEstimate(flops=4_000_000_000, bytes_accessed=13_000_000, transcendentals=300_000),
    )(tile_counts, block_rows[0], block_cols[0], features, weight, cotangent, blocks)
    return pl.pallas_call(
        write_out,
        out_shape=(
            jax.ShapeDtypeStruct(features.shape, BF),
            jax.ShapeDtypeStruct(features.shape, BF),
            jax.ShapeDtypeStruct((FS, 512), F32),
        ),
        in_specs=[vm] * 3,
        out_specs=(vm, vm, vm),
        cost_estimate=pl.CostEstimate(flops=0, bytes_accessed=2_000_000, transcendentals=0),
    )(act_t, gf_t, grad_weight)


def solution(mesh):
    in_specs = (
        P(("row", "col"), "depth"),
        P(),
        P(("row", "col"), "depth"),
        P("row", "col", None, None, None),
        P("row", "col", None),
        P("row", "col", None),
        P("row", "col"),
    )
    out_specs = (P(("row", "col"), "depth"), P(("row", "col"), "depth"), P("depth", None))
    return jax.shard_map(layer, mesh=mesh, in_specs=in_specs, out_specs=out_specs, check_vma=False)
```

time: 170 us -> 139 us (0.82)
  Pallas kernels: 157 us -> 136 us
  local copies, waits for them, and re-layouts: 5.68 us -> 0 us
  other arithmetic: 5 us -> 0 us
    pallas_call x1 -> x2, Pallas kernels: 157 us -> 136 us  [the longest x1 134 us: layer(): pl.pallas_call(kernel, out_shape=(jax.ShapeDtypeStruct((4, FS, BS), BF),...]
    unnamed x3 -> x0, local copies, waits for them, and re-layouts: 5.01 us -> none
    reduce_sum x4 -> x0, other arithmetic: 2.61 us -> none  [the longest x2 1.55 us: sorted_slots(): jnp.sum((valid[None, :] & (major[None, :] <= g[:, None])).astype(jnp.int3...]
where the time goes in v2:
time: 139 us; the launch traced here: 137 us
  Pallas kernels  136 us (98%)
    pallas_call x1, Pallas kernels, layer(): pl.pallas_call(kernel, out_shape=(jax.ShapeDtypeStruct((4, FS, BS), BF),...  134 us

profile of v2, /device:TPU:8, one launch (start us, length us, event | category | flops | bytes accessed | tf_op | source)
XLA Modules:
  0.0 137.3 jit_solution(12095777740517182040)
XLA Ops:
  1.3 133.7 %shard_map.94 = (bf16[4,128,256]{2,1,0:T(8,128)(2,1)}, f32[4,128,256]{2,1,0:T(8,128)}, f32[128,512]{1,0:T(8,128)}) custom-call(s32[1,1]{1,0:T(1,128)S(6)} %copy.10.count, s32[1,80]{1,0:T(1,128)} %bitcast.4, s32[1,80]{1,0:T(1,128)} %bitcast.5, bf16[1024,128]{1,0:T(8,128)(2,1)} %feat.1, bf16[512,512]{1,0:T(8,128)(2,1)} %weight.1, bf16[1024,128]{1,0:T(8,128)(2,1)} %cot.1, ...), custom_call_target="tpu_custom_call" | custom-call | flops 4000000000 | bytes 13000000 | tf_op jit(solution)/shard_map/pallas_call | solution.py:771
  135.0 2.3 %shard_map.95 = (bf16[1024,128]{1,0:T(8,128)(2,1)}, bf16[1024,128]{1,0:T(8,128)(2,1)}, f32[128,512]{1,0:T(8,128)}) custom-call(bf16[4,128,256]{2,1,0:T(8,128)(2,1)} %get-tuple-element.6.act_t, f32[4,128,256]{2,1,0:T(8,128)} %get-tuple-element.7.gf_t, f32[128,512]{1,0:T(8,128)} %get-tuple-element.8.gw), custom_call_target="tpu_custom_call" | custom-call | bytes 2000000 | tf_op jit(solution)/shard_map/pallas_call | solution.py:786

commit v3 on v2

--- a/solution.py
+++ b/solution.py
@@ -136,29 +136,37 @@
         go(op, shard(k, x, zz), shard(k, x, zz), xsr.at[k, zz], xrl.at[k, zz], right)
         go(op, shard(k, x, zz), shard(k, x, zz), xsl.at[k, zz], xrr.at[k, zz], left)
 
-    def z_stage(op, k):
+    def z_stage(op, first, count=1):
         for o in range(1, 4):
             @pl.when(z >= o)
             def _():
                 zz = z - o
-                if op == "start":
-                    z_up("recv", k, zz)
-
-                @pl.when(z < 3)
-                def _():
-                    z_up(op, k, zz)
-                x_send(op, k, zz)
+
+                def one(k, _):
+                    if op == "start":
+                        z_up("recv", k, zz)
+
+                    @pl.when(z < 3)
+                    def _():
+                        z_up(op, k, zz)
+                    x_send(op, k, zz)
+                    return 0
+                lax.fori_loop(first, first + count, one, 0)
 
             @pl.when(z + o <= 3)
             def _():
                 zz = z + o
-                if op == "start":
-                    z_down("recv", k, zz)
-
-                @pl.when(z > 0)
-                def _():
-                    z_down(op, k, zz)
-                x_send(op, k, zz)
+
+                def one(k, _):
+                    if op == "start":
+                        z_down("recv", k, zz)
+
+                    @pl.when(z > 0)
+                    def _():
+                        z_down(op, k, zz)
+                    x_send(op, k, zz)
+                    return 0
+                lax.fori_loop(first, first + count, one, 0)
 
     def x_pass(op, k):
         def one(i, _):
@@ -244,7 +252,7 @@
             acc = acc * idx[KF, s].astype(F32) + prod
             buf[s] = acc.astype(BF)
             return acc
-        lax.fori_loop(0, NB, slot, jnp.zeros((CH, BS), F32), unroll=8)
+        lax.fori_loop(0, NB, slot, jnp.zeros((CH, BS), F32), unroll=16)
 
         def pick(p, _):
             for q in range(4):
@@ -273,11 +281,9 @@
     idx_copy = pltpu.make_async_copy(table, idx, idx_sem)
     idx_copy.start()
 
-    z_stage("start", 0)
     for b in range(4):
         cott[zh, b] = cot[b * BS:(b + 1) * BS, :].astype(F32).T.astype(BF)
-    if K > 1:
-        z_stage("start", 1)
+    z_stage("start", 0, K)
     if K == 2:
         cot_send("start")
     for i in range(2):
@@ -492,7 +498,7 @@
             acc = acc * idx[KB, s].astype(F32) + prod
             buf[s] = acc.astype(BF)
             return acc
-        lax.fori_loop(0, NB, slot, jnp.zeros((CH, BS), F32), unroll=8)
+        lax.fori_loop(0, NB, slot, jnp.zeros((CH, BS), F32), unroll=16)
 
         def pick(i, _):
             last = idx[LB, i]
@@ -684,15 +690,6 @@
     finish(0)
     finish3(1)
     weight_step(4)
-    x_sum(1)
-    pass_on("start", 1)
-    finish(1)
-
-    for o in range(1, 4):
-        src = (c + o) % 4
-        ref = gw_out.at[pl.ds(pl.multiple_of(src * 32, 32), 32), :]
-        go("recv", ref, ref, vys.at[o], vyr.at[src], {"col": src})
-
     def drain(k, _):
         z_own("sent", k)
         x_send("sent", k, z)
@@ -701,19 +698,33 @@
         for fn in (y_send, d_send, d_pass, t_send):
             blocks(fn, "sent", k)
         far_half("sent", k)
-        near_full("sent", k)
-        x_sum_sent(k)
-        pass_on("sent", k)
         for stage in range(3):
             line3("sent", k, stage)
         far3("sent", k)
         near3("sent", k)
         return 0
     lax.fori_loop(0, K, drain, 0)
+    near_full("sent", 0)
+    x_sum_sent(0)
+    pass_on("sent", 0)
     blocks(mix_send, "sent")
     cot_send("sent")
-    for fn in (wy, wx, wz, vx, vy):
+    for fn in (wy, wx, wz, vx):
         all3(fn, "sent")
+
+    x_sum(1)
+    pass_on("start", 1)
+    finish(1)
+
+    for o in range(1, 4):
+        src = (c + o) % 4
+        ref = gw_out.at[pl.ds(pl.multiple_of(src * 32, 32), 32), :]
+        go("recv", ref, ref, vys.at[o], vyr.at[src], {"col": src})
+
+    near_full("sent", K - 1)
+    x_sum_sent(K - 1)
+    pass_on("sent", K - 1)
+    all3(vy, "sent")
 
 
 def write_out(act_t, gf_t, gw, act, gf, gw_out):

time: 139 us -> 135 us (0.971)
  Pallas kernels: 136 us -> 132 us
    pallas_call x1, Pallas kernels: 134 us -> 130 us  [layer(): pl.pallas_call(kernel, out_shape=(jax.ShapeDtypeStruct((4, FS, BS), BF),...]
where the time goes in v3:
time: 135 us; the launch traced here: 134 us
  Pallas kernels  132 us (98%)
    pallas_call x1, Pallas kernels, layer(): pl.pallas_call(kernel, out_shape=(jax.ShapeDtypeStruct((4, FS, BS), BF),...  130 us

profile of v3, /device:TPU:8, one launch (start us, length us, event | category | flops | bytes accessed | tf_op | source)
XLA Modules:
  0.0 133.5 jit_solution(5980228242077068965)
XLA Ops:
  1.3 130.0 %shard_map.94 = (bf16[4,128,256]{2,1,0:T(8,128)(2,1)}, f32[4,128,256]{2,1,0:T(8,128)}, f32[128,512]{1,0:T(8,128)}) custom-call(s32[1,1]{1,0:T(1,128)S(6)} %copy.10.count, s32[1,80]{1,0:T(1,128)} %bitcast.4, s32[1,80]{1,0:T(1,128)} %bitcast.5, bf16[1024,128]{1,0:T(8,128)(2,1)} %feat.1, bf16[512,512]{1,0:T(8,128)(2,1)} %weight.1, bf16[1024,128]{1,0:T(8,128)(2,1)} %cot.1, ...), custom_call_target="tpu_custom_call" | custom-call | flops 4000000000 | bytes 13000000 | tf_op jit(solution)/shard_map/pallas_call | solution.py:782
  131.3 2.3 %shard_map.95 = (bf16[1024,128]{1,0:T(8,128)(2,1)}, bf16[1024,128]{1,0:T(8,128)(2,1)}, f32[128,512]{1,0:T(8,128)}) custom-call(bf16[4,128,256]{2,1,0:T(8,128)(2,1)} %get-tuple-element.6.act_t, f32[4,128,256]{2,1,0:T(8,128)} %get-tuple-element.7.gf_t, f32[128,512]{1,0:T(8,128)} %get-tuple-element.8.gw), custom_call_target="tpu_custom_call" | custom-call | bytes 2000000 | tf_op jit(solution)/shard_map/pallas_call | solution.py:797

commit v4 on v3

--- a/solution.py
+++ b/solution.py
@@ -284,13 +284,12 @@
     for b in range(4):
         cott[zh, b] = cot[b * BS:(b + 1) * BS, :].astype(F32).T.astype(BF)
     z_stage("start", 0, K)
-    if K == 2:
-        cot_send("start")
     for i in range(2):
         for j in range(4):
             cols = pl.ds(pl.multiple_of((i * 2 + core) * FS, FS), FS)
             wt[i, :, j * FS:(j + 1) * FS] = weight[j * FS:(j + 1) * FS, cols].astype(F32).T.astype(BF)
     x_pass("start", 0)
+    cot_send("start")
     idx_copy.wait()
     adj_copy.wait()
 
@@ -319,10 +318,6 @@
         x_last(k)
 
         forward_tile(k)
-
-        @pl.when(k > 0)
-        def _():
-            blocks(d_pass, "start", k - 1)
         return 0
     lax.fori_loop(0, K, forward_step, 0)
 
@@ -331,6 +326,7 @@
         d_send("start", K - 1, p)
         return 0
     lax.fori_loop(0, NP, last_sum, 0)
+    blocks(d_pass, "start", K - 2)
     go("recv", cott.at[1 - zh], cott.at[1 - zh], cs.at[0], cr.at[0], to_far)
 
     def mix_rows(p, dd):

time: 135 us -> 133 us (0.985)
  no operation moved by 1% of the time
where the time goes in v4:
time: 133 us; the launch traced here: 132 us
  Pallas kernels  131 us (98%)
    pallas_call x1, Pallas kernels, layer(): pl.pallas_call(kernel, out_shape=(jax.ShapeDtypeStruct((4, FS, BS), BF),...  129 us

profile of v4, /device:TPU:8, one launch (start us, length us, event | category | flops | bytes accessed | tf_op | source)
XLA Modules:
  0.0 132.2 jit_solution(10783108856359855022)
XLA Ops:
  1.3 128.7 %shard_map.94 = (bf16[4,128,256]{2,1,0:T(8,128)(2,1)}, f32[4,128,256]{2,1,0:T(8,128)}, f32[128,512]{1,0:T(8,128)}) custom-call(s32[1,1]{1,0:T(1,128)S(6)} %copy.10.count, s32[1,80]{1,0:T(1,128)} %bitcast.4, s32[1,80]{1,0:T(1,128)} %bitcast.5, bf16[1024,128]{1,0:T(8,128)(2,1)} %feat.1, bf16[512,512]{1,0:T(8,128)(2,1)} %weight.1, bf16[1024,128]{1,0:T(8,128)(2,1)} %cot.1, ...), custom_call_target="tpu_custom_call" | custom-call | flops 4000000000 | bytes 13000000 | tf_op jit(solution)/shard_map/pallas_call | solution.py:778
  130.0 2.3 %shard_map.95 = (bf16[1024,128]{1,0:T(8,128)(2,1)}, bf16[1024,128]{1,0:T(8,128)(2,1)}, f32[128,512]{1,0:T(8,128)}) custom-call(bf16[4,128,256]{2,1,0:T(8,128)(2,1)} %get-tuple-element.6.act_t, f32[4,128,256]{2,1,0:T(8,128)} %get-tuple-element.7.gf_t, f32[128,512]{1,0:T(8,128)} %get-tuple-element.8.gw), custom_call_target="tpu_custom_call" | custom-call | bytes 2000000 | tf_op jit(solution)/shard_map/pallas_call | solution.py:793
